TPU v7x, 32 devices: a whole 2x2x4 slice. The times are simulated.
32 devices in a mesh: row: 4 (over y, x), col: 8 (over z, core).
Axes of the slice: x: 2, y: 2, z: 4, core: 2. Of those that a mesh axis runs over, the one named last changes fastest.
Arguments:
- resid_in: bfloat16 [1024, 4096], P('col', 'row'), may hold values from -6 to 6
- attn_out: bfloat16 [1024, 4096], P('row', 'col'), may hold values from -6 to 6
- cotangent: bfloat16 [1024, 4096], P('col', 'row'), may hold values from -6 to 6
- w_out: bfloat16 [4096, 4096], P('col', 'row'), may hold values from -0.09375 to 0.09375
- w_gate: bfloat16 [4096, 16384], P('row', 'col'), may hold values from -0.09375 to 0.09375
- w_up: bfloat16 [4096, 16384], P('row', 'col'), may hold values from -0.09375 to 0.09375
- w_down: bfloat16 [16384, 4096], P('col', 'row'), may hold values from -0.046875 to 0.046875
- mask_out: int32 [32, 32], P('col', 'row'), may hold values 0 or 1
- mask_gate: int32 [32, 128], P('row', 'col'), may hold values 0 or 1
- mask_up: int32 [32, 128], P('row', 'col'), may hold values 0 or 1
- mask_down: int32 [128, 32], P('col', 'row'), may hold values 0 or 1
Outputs:
- layer_out: bfloat16 [1024, 4096], P('col', 'row')
- grad_resid: bfloat16 [1024, 4096], P('col', 'row')
- grad_attn: bfloat16 [1024, 4096], P('row', 'col')
- grad_w_out: bfloat16 [4096, 4096], P('col', 'row')
- grad_w_gate: bfloat16 [4096, 16384], P('row', 'col')
- grad_w_up: bfloat16 [4096, 16384], P('row', 'col')
- grad_w_down: bfloat16 [16384, 4096], P('col', 'row')
All inputs are finite; a program needn't handle non-finite values. No bound on the sum of `mask_out` or of `mask_gate` or of `mask_up` or of `mask_down` on one device may be relied on, other than what follows from the above.
Results may differ from a plain program's by a relative error of at most 0.0068.
Values may be sent and summed in bfloat16 or wider, within the bound.
A program may use at most 192 MiB of HBM per device.

v0:
```python
import jax
import jax.numpy as jnp
from jax import lax
from jax.sharding import PartitionSpec as P

BLOCK = 128


def expand(weight, flags):
    blocks_r = weight.shape[0] // BLOCK
    blocks_c = weight.shape[1] // BLOCK
    shaped = weight.reshape(blocks_r, BLOCK, blocks_c, BLOCK)
    return (shaped * flags.astype(weight.dtype)[:, None, :, None]).reshape(weight.shape)


def product_nn(left, right):
    return jnp.dot(left, right, preferred_element_type=jnp.float32)


def product_nt(left, right):
    return lax.dot_general(
        left, right, (((1,), (1,)), ((), ())), preferred_element_type=jnp.float32
    )


def product_tn(left, right):
    return lax.dot_general(
        left, right, (((0,), (0,)), ((), ())), preferred_element_type=jnp.float32
    )


def row_gather(value):
    return lax.all_gather(value, "row", axis=0, tiled=True)


def col_gather(value):
    return lax.all_gather(value, "col", axis=0, tiled=True)


def row_sum(panel, weight):
    return lax.psum_scatter(product_nt(panel, weight), "row", scatter_dimension=0, tiled=True)


def col_sum(panel, weight, transposed):

    def col_term():
        if transposed:
            return product_nt(panel, weight)
        return product_nn(panel, weight)

    return lax.psum_scatter(col_term(), "col", scatter_dimension=0, tiled=True)


def local(
    resid_in,
    attn_out,
    cotangent,
    w_out,
    w_gate,
    w_up,
    w_down,
    mask_out,
    mask_gate,
    mask_up,
    mask_down,
):
    f32 = jnp.float32
    pruned_out = expand(w_out, mask_out)
    pruned_gate = expand(w_gate, mask_gate)
    pruned_up = expand(w_up, mask_up)
    pruned_down = expand(w_down, mask_down)
    units = pruned_gate.shape[1]
    w_pair = jnp.concatenate([pruned_gate, pruned_up], 1)
    attn_full = row_gather(attn_out)
    projected = col_sum(attn_full, pruned_out, False)
    resid = (resid_in.astype(f32) + projected).astype(jnp.bfloat16)
    resid_full = col_gather(resid)
    pair_val = lax.psum_scatter(
        product_nn(resid_full, w_pair), "row", scatter_dimension=0, tiled=True
    )
    gate_val = pair_val[:, :units]
    up_val = pair_val[:, units:]
    logistic = jax.nn.sigmoid(gate_val)
    hidden = (gate_val * logistic * up_val).astype(jnp.bfloat16)
    hidden_full = lax.all_gather(hidden, "row", axis=0, tiled=True)
    lowered = col_sum(hidden_full, pruned_down, False)
    layer_out = (resid.astype(f32) + lowered).astype(jnp.bfloat16)
    upstream = col_gather(cotangent)
    hidden_grad = row_sum(upstream, pruned_down)
    gate_grad = (hidden_grad * up_val * logistic * (1.0 + gate_val * (1.0 - logistic))).astype(
        jnp.bfloat16
    )
    up_grad = (hidden_grad * gate_val * logistic).astype(jnp.bfloat16)
    pair_grad = row_gather(jnp.concatenate([gate_grad, up_grad], 1))
    grad_w_down = expand(product_tn(hidden_full, upstream), mask_down).astype(jnp.bfloat16)
    pair_weight_grad = product_tn(resid_full, pair_grad)
    grad_w_gate = expand(pair_weight_grad[:, :units], mask_gate).astype(jnp.bfloat16)
    grad_w_up = expand(pair_weight_grad[:, units:], mask_up).astype(jnp.bfloat16)
    returned = col_sum(pair_grad, w_pair, True)
    grad_resid = (cotangent.astype(f32) + returned).astype(jnp.bfloat16)
    grad_full = col_gather(grad_resid)
    grad_attn = row_sum(grad_full, pruned_out).astype(jnp.bfloat16)
    grad_w_out = expand(product_tn(attn_full, grad_full), mask_out).astype(jnp.bfloat16)
    return (layer_out, grad_resid, grad_attn, grad_w_out, grad_w_gate, grad_w_up, grad_w_down)


def solution(mesh):
    placed = (
        P("col", "row"),
        P("row", "col"),
        P("col", "row"),
        P("col", "row"),
        P("row", "col"),
        P("row", "col"),
        P("col", "row"),
        P("col", "row"),
        P("row", "col"),
        P("row", "col"),
        P("col", "row"),
    )
    return jax.shard_map(
        local,
        mesh=mesh,
        in_specs=placed,
        out_specs=(
            P("col", "row"),
            P("col", "row"),
            P("row", "col"),
            P("col", "row"),
            P("row", "col"),
            P("row", "col"),
            P("col", "row"),
        ),
        check_vma=False,
    )
```

profile of v0, /device:TPU:0, one launch (start us, length us, event | category | flops | bytes accessed | tf_op | source)
XLA Modules:
  0.0 742.8 jit_solution(9669921474161339583)
XLA Ops:
  7.2 0.7 all-gather.7.cloned.1.call-update
  7.9 0.8 fusion.13
  8.7 30.5 %all-gather.7.cloned.1.call-done = bf16[1024,512]{1,0:T(8,128)(2,1)} async-done(((bf16[256,512]{1,0:T(8,128)(2,1)}), bf16[1024,512]{1,0:T(8,128)(2,1)}) %all-gather.7.cloned.1.call-update) | async-done | bytes 1048592 | tf_op jit(solution)/shard_map/all_gather | solution.py:33
  39.4 4.9 convolution_bitcast_fusion.1
  44.4 0.7 all-gather.13.cloned.1.call-update
  45.4 49.1 %reduce-scatter.7.cloned.1.call-done = f32[128,1024]{0,1:T(8,128)} async-done(((f32[1024,1024]{0,1:T(8,128)}), f32[128,1024]{0,1:T(8,128)}) %reduce-scatter.7.cloned.1.call-update) | async-done | bytes 524304 | tf_op jit(solution)/shard_map/reduce_scatter | solution.py:51
  94.5 1.8 add_convert_fusion.2
  96.5 26.9 %all-gather.13.cloned.1.call-done = bf16[1024,1024]{1,0:T(8,128)(2,1)} async-done(((bf16[128,1024]{1,0:T(8,128)(2,1)}), bf16[1024,1024]{1,0:T(8,128)(2,1)}) %all-gather.13.cloned.1.call-update) | async-done | bytes 2097168 | tf_op jit(solution)/shard_map/all_gather | solution.py:37
  123.4 0.6 mul.123
  124.0 2.1 copy-done
  126.1 0.9 copy-done.10
  127.1 8.6 %convolution_bitcast_fusion = f32[1024,2048]{1,0:T(8,128)} fusion(bf16[1024,1024]{1,0:T(8,128)(2,1)} %all-gather.13.cloned.1.call-done, bf16[2048,1024]{1,0:T(8,128)(2,1)S(1)} %copy-done.10, bf16[256,8,8,128]{3,2,1,0:T(8,128)(2,1)S(1)} %bitcast.71), kind=kOutput, calls=%fused_computation.9 | convolution fusion | flops 4297064448 | bytes 18874368 | tf_op jit(solution)/shard_map/dot_general | solution.py:21
  135.8 0.6 copy-done.8
  136.4 0.6 mul.118
  137.0 0.6 mul.115
  137.6 0.9 copy-done.1
  138.6 1.3 copy-done.2
  139.8 4.3 bitcast_multiply_fusion.4
  144.1 11.6 %all-gather.9.cloned.1.call-done = bf16[1024,1024]{0,1:T(8,128)(2,1)} async-done(((bf16[128,1024]{0,1:T(8,128)(2,1)}), bf16[1024,1024]{0,1:T(8,128)(2,1)}) %all-gather.9.cloned.1.call-update) | async-done | bytes 2097168 | tf_op jit(solution)/shard_map/all_gather | solution.py:37
  155.7 16.2 %fusion.4 = f32[1024,4096]{1,0:T(8,128)} fusion(bf16[1024,1024]{0,1:T(8,128)(2,1)} %all-gather.9.cloned.1.call-done, bf16[1024,2048]{1,0:T(8,128)(2,1)} %get-tuple-element.27, bf16[1024,2048]{1,0:T(8,128)(2,1)} %get-tuple-element.28), kind=kOutput, calls=%fused_computation.8 | convolution fusion | flops 8606711808 | bytes 27262976 | tf_op jit(solution)/shard_map/dot_general | solution.py:17
  172.2 71.9 %reduce-scatter.13.cloned.1.call-done = f32[256,2048]{1,0:T(8,128)} async-done(((f32[1024,2048]{1,0:T(8,128)}), f32[256,2048]{1,0:T(8,128)}) %reduce-scatter.13.cloned.1.call-update) | async-done | bytes 2097168 | tf_op jit(solution)/shard_map/reduce_scatter | solution.py:41
  244.2 157.1 %reduce-scatter.9.cloned.1.call-done = f32[256,4096]{1,0:T(8,128)} async-done(((f32[1024,4096]{1,0:T(8,128)}), f32[256,4096]{1,0:T(8,128)}) %reduce-scatter.9.cloned.1.call-update) | async-done | bytes 4194320 | tf_op jit(solution)/shard_map/reduce_scatter | solution.py:78
  401.2 5.2 multiply_convert_fusion.1
  406.4 1.6 pad_maximum_fusion.3
  408.1 87.7 %all-gather.15.cloned.1.call-done = bf16[1024,4096]{1,0:T(8,128)(2,1)} async-done(((bf16[256,4096]{1,0:T(8,128)(2,1)}), bf16[1024,4096]{1,0:T(8,128)(2,1)}) %all-gather.15.cloned.1.call-update) | async-done | bytes 8388624 | tf_op jit(solution)/shard_map/all_gather | solution.py:33
  495.8 15.1 %fusion.3 = f32[1024,1024]{1,0:T(8,128)} fusion(bf16[1024,4096]{1,0:T(8,128)(2,1)} %all-gather.15.cloned.1.call-done, bf16[1024,2048]{1,0:T(8,128)(2,1)} %get-tuple-element.27, bf16[1024,2048]{1,0:T(8,128)(2,1)} %get-tuple-element.28), kind=kOutput, calls=%fused_computation.7 | convolution fusion | flops 8606711808 | bytes 20971520 | tf_op jit(solution)/shard_map/dot_general | solution.py:21
  511.0 0.7 all-gather.11.cloned.1.call-update
  511.7 49.4 %reduce-scatter.15.cloned.1.call-done = f32[128,1024]{1,0:T(8,128)} async-done(((f32[1024,1024]{1,0:T(8,128)}), f32[128,1024]{1,0:T(8,128)}) %reduce-scatter.15.cloned.1.call-update) | async-done | bytes 524304 | tf_op jit(solution)/shard_map/reduce_scatter | solution.py:51
  561.1 1.8 add_convert_fusion
  563.0 51.6 %all-gather.11.cloned.1.call-done = bf16[1024,2048]{1,0:T(8,128)(2,1)} async-done(((bf16[256,2048]{1,0:T(8,128)(2,1)}), bf16[1024,2048]{1,0:T(8,128)(2,1)}) %all-gather.11.cloned.1.call-update) | async-done | bytes 4194320 | tf_op jit(solution)/shard_map/all_gather | solution.py:85
  614.6 11.3 %fusion.6 = f32[1024,1024]{0,1:T(8,128)} fusion(bf16[1024,2048]{1,0:T(8,128)(2,1)} %all-gather.11.cloned.1.call-done, bf16[2048,1024]{1,0:T(8,128)(2,1)} %param.17, bf16[256,8,8,128]{3,2,1,0:T(8,128)(2,1)} %bitcast.72), kind=kOutput, calls=%fused_computation.21 | convolution fusion | flops 4297064448 | bytes 16777216 | tf_op jit(solution)/shard_map/dot_general | solution.py:17
  626.1 19.7 %all-gather.17.cloned.1.call-done = bf16[1024,1024]{1,0:T(8,128)(2,1)} async-done(((bf16[128,1024]{1,0:T(8,128)(2,1)}), bf16[1024,1024]{1,0:T(8,128)(2,1)}) %all-gather.17.cloned.1.call-update) | async-done | bytes 2097168 | tf_op jit(solution)/shard_map/all_gather | solution.py:37
  645.8 4.2 fusion.7
  650.1 0.6 mul.141
  650.7 1.6 copy-done.11
  652.3 8.9 %fusion = bf16[2048,1024]{1,0:T(8,128)(2,1)} fusion(f32[256,8,8,128]{3,2,1,0:T(8,128)S(1)} %bitcast.68, bf16[1024,2048]{1,0:T(8,128)(2,1)S(1)} %copy-done.11, bf16[1024,1024]{1,0:T(8,128)(2,1)} %all-gather.13.cloned.1.call-done), kind=kOutput, calls=%fused_computation.1 | convolution fusion | flops 4299161600 | bytes 18874368 | tf_op jit(solution)/shard_map/dot_general | solution.py:27
  661.2 11.6 %fusion.14 = f32[1024,4096]{1,0:T(8,128)} fusion(bf16[1024,1024]{0,1:T(8,128)(2,1)S(1)} %copy-done.12, bf16[1024,4096]{1,0:T(8,128)(2,1)S(1)} %bitcast.75), kind=kOutput, calls=%fused_computation.33 | convolution fusion | flops 8589934592 | bytes 27262976 | tf_op jit(solution)/shard_map/dot_general | solution.py:27
  672.8 0.6 mul.138
  673.4 3.9 mul.135
  677.3 14.2 %fusion.1 = (bf16[1024,2048]{1,0:T(8,128)(2,1)}, bf16[1024,2048]{1,0:T(8,128)(2,1)}) fusion(f32[128,8,16,128]{3,2,1,0:T(8,128)S(1)} %bitcast.64, f32[1024,4096]{1,0:T(8,128)} %fusion.14, f32[128,8,16,128]{3,2,1,0:T(8,128)} %bitcast.65), kind=kLoop, calls=%fused_computation.3 | loop fusion | flops 8388608 | bytes 41943040 | tf_op jit(solution)/shard_map/convert_element_type | solution.py:98
  691.5 6.2 reduce-scatter.11.cloned.1.call-done
  697.8 1.1 add_convert_fusion.1
  698.8 0.8 copy.24
  699.7 0.3 mul.132
  700.0 3.1 fusion.5
  703.2 1.3 copy.25
  704.5 29.7 %reduce-scatter.17.cloned.1.call-done = f32[256,512]{1,0:T(8,128)} async-done(((f32[1024,512]{1,0:T(8,128)}), f32[256,512]{1,0:T(8,128)}) %reduce-scatter.17.cloned.1.call-update) | async-done | bytes 524304 | tf_op jit(solution)/shard_map/reduce_scatter | solution.py:41
  734.2 1.8 convert_element_type.79
  (54 shorter events, 1.6 us)
Async XLA Ops:
  7.2 32.0 %all-gather.7.cloned.1.call-start = ((), (), s32[]{:S(2)}) async-start(), calls=%async_computation.6 | async-start | bytes 1310720 | tf_op jit(solution)/shard_map/all_gather | solution.py:33
  7.9 86.6 %reduce-scatter.7.cloned.1.call-start = ((), (), s32[]{:S(2)}) async-start(), calls=%async_computation.7 | async-start | bytes 4718592 | tf_op jit(solution)/shard_map/reduce_scatter | solution.py:51
  44.3 0.9 copy-start.6
  44.3 52.1 %copy-start.7 = (s32[16,8]{0,1:T(8,128)S(1)}, s32[16,8]{0,1:T(8,128)}, u32[]{:S(2)}) copy-start(s32[16,8]{0,1:T(8,128)} %param.21) | copy-start | bytes 1540
  44.3 79.0 %all-gather.13.cloned.1.call-start = ((), (), s32[]{:S(2)}) async-start(), calls=%async_computation.12 | async-start | bytes 2359296 | tf_op jit(solution)/shard_map/all_gather | solution.py:37
  45.1 110.7 %all-gather.9.cloned.1.call-start = ((), (), s32[]{:S(2)}) async-start(), calls=%async_computation.8 | async-start | bytes 2359296 | tf_op jit(solution)/shard_map/all_gather | solution.py:37
  96.3 147.8 %reduce-scatter.13.cloned.1.call-start = ((), (), s32[]{:S(2)}) async-start(), calls=%async_computation.13 | async-start | bytes 10485760 | tf_op jit(solution)/shard_map/reduce_scatter | solution.py:41
  123.4 3.7 copy-start.10
  124.0 2.1 copy-start
  135.7 0.7 copy-start.8
  135.7 0.7 copy-start.9
  135.7 265.5 %reduce-scatter.9.cloned.1.call-start = ((), (), s32[]{:S(2)}) async-start(), calls=%async_computation.9 | async-start | bytes 20971520 | tf_op jit(solution)/shard_map/reduce_scatter | solution.py:78
  136.4 2.2 copy-start.1
  136.4 3.5 copy-start.2
  172.0 323.8 %all-gather.15.cloned.1.call-start = ((), (), s32[]{:S(2)}) async-start(), calls=%async_computation.14 | async-start | bytes 10485760 | tf_op jit(solution)/shard_map/all_gather | solution.py:33
  408.0 153.1 %reduce-scatter.15.cloned.1.call-start = ((), (), s32[]{:S(2)}) async-start(), calls=%async_computation.15 | async-start | bytes 4718592 | tf_op jit(solution)/shard_map/reduce_scatter | solution.py:51
  510.9 50.2 %copy-start.5 = (bf16[128,1024]{1,0:T(8,128)(2,1)S(1)}, bf16[128,1024]{1,0:T(8,128)(2,1)}, u32[]{:S(2)}) copy-start(bf16[128,1024]{1,0:T(8,128)(2,1)} %param.13) | copy-start | bytes 786436
  510.9 103.6 %all-gather.11.cloned.1.call-start = ((), (), s32[]{:S(2)}) async-start(), calls=%async_computation.10 | async-start | bytes 5242880 | tf_op jit(solution)/shard_map/all_gather | solution.py:85
  511.7 134.1 %all-gather.17.cloned.1.call-start = ((), (), s32[]{:S(2)}) async-start(), calls=%async_computation.16 | async-start | bytes 2359296 | tf_op jit(solution)/shard_map/all_gather | solution.py:37
  562.9 134.8 %reduce-scatter.11.cloned.1.call-start = ((), (), s32[]{:S(2)}) async-start(), calls=%async_computation.11 | async-start | bytes 4718592 | tf_op jit(solution)/shard_map/reduce_scatter | solution.py:51
  625.9 19.9 %copy-start.4 = (bf16[512,1024]{1,0:T(8,128)(2,1)S(1)}, bf16[512,1024]{1,0:T(8,128)(2,1)}, u32[]{:S(2)}) copy-start(bf16[512,1024]{1,0:T(8,128)(2,1)} %param.14) | copy-start | bytes 3145732
  625.9 108.3 %reduce-scatter.17.cloned.1.call-start = ((), (), s32[]{:S(2)}) async-start(), calls=%async_computation.17 | async-start | bytes 2621440 | tf_op jit(solution)/shard_map/reduce_scatter | solution.py:41
  650.1 2.2 copy-start.11
  650.1 11.1 %slice-start = ((s8[8388608]{0:T(1024)(128)(4,1)}), s8[4194304]{0:T(1024)(128)(4,1)S(1)}, s32[]{:S(2)}) async-start(s8[8388608]{0:T(1024)(128)(4,1)} %bitcast.74), calls=%async_computation.18 | async-start | bytes 8388608
  652.3 8.9 %slice-start.1 = ((s8[8388608]{0:T(1024)(128)(4,1)}), s8[4194304]{0:T(1024)(128)(4,1)S(1)}, s32[]{:S(2)}) async-start(s8[8388608]{0:T(1024)(128)(4,1)} %bitcast.74), calls=%async_computation.19 | async-start | bytes 8388608
  652.3 8.9 %copy-start.12 = (bf16[1024,1024]{0,1:T(8,128)(2,1)S(1)}, bf16[1024,1024]{0,1:T(8,128)(2,1)}, u32[]{:S(2)}) copy-start(bf16[1024,1024]{0,1:T(8,128)(2,1)} %all-gather.9.cloned.1.call-done) | copy-start | bytes 6291460
  677.3 20.4 %copy-start.3 = (bf16[128,1024]{0,1:T(8,128)(2,1)S(1)}, bf16[128,1024]{0,1:T(8,128)(2,1)}, u32[]{:S(2)}) copy-start(bf16[128,1024]{0,1:T(8,128)(2,1)} %add_convert_fusion.2) | copy-start | bytes 786436
Sparse Core Ops, SparseCore 0:
  9.8 29.3 all-gather.6
  44.4 49.9 reduce-scatter.6
  96.1 27.2 all-gather.12
  125.4 30.3 all-gather.8
  158.7 85.4 reduce-scatter.12
  247.4 153.7 reduce-scatter.8
  408.2 87.5 all-gather.14
  511.1 49.9 reduce-scatter.14
  563.7 50.8 all-gather.10
  616.7 29.0 all-gather.16
  648.2 49.4 reduce-scatter.10
  700.8 33.3 reduce-scatter.16
where the time goes:
time: 743 us
  waiting for transfers between devices  594 us (80%)
  matrix products  84 us (11%)
  other arithmetic  32.5 us (4%)
  local copies, waits for them, and re-layouts  17.7 us (2%)
  between operations  14.4 us (2%)
    reduce_scatter x1, waiting for transfers between devices, local(): lax.psum_scatter(product_nn(resid_full, w_pair), 'row', scatter_dimension...  157 us
    all_gather x2, waiting for transfers between devices, row_gather(): return lax.all_gather(value, 'row', axis=0, tiled=True)  118 us
    reduce_scatter x3, waiting for transfers between devices, col_sum(): return lax.psum_scatter(col_term(), 'col', scatter_dimension=0, tiled=True)  105 us
    reduce_scatter x2, waiting for transfers between devices, row_sum(): lax.psum_scatter(product_nt(panel, weight), 'row', scatter_dimension=0, t...  102 us
    all_gather x3, waiting for transfers between devices, col_gather(): return lax.all_gather(value, 'col', axis=0, tiled=True)  58.2 us
    all_gather x1, waiting for transfers between devices, local(): hidden_full = lax.all_gather(hidden, 'row', axis=0, tiled=True)  51.6 us
    dot_general x3, matrix products, product_nn(): return jnp.dot(left, right, preferred_element_type=jnp.float32)  32.4 us
    dot_general x3, matrix products, product_nt(): lax.dot_general(left, right, (((1,), (1,)), ((), ())), preferred_element_...  28 us
  transfers between devices with their start and end apart: 12, of which 12 were waited for; matrix products, arithmetic and copies ran while one was open for 13% of the time, Pallas kernels for 0%

commit v1 on v0

v1 whole, which is shorter than its diff:
```python
import jax
import jax.numpy as jnp
from jax import lax
from jax.sharding import PartitionSpec as P

BLOCK = 128
CHUNKS = 2


def expand(weight, flags):
    blocks_r = weight.shape[0] // BLOCK
    blocks_c = weight.shape[1] // BLOCK
    shaped = weight.reshape(blocks_r, BLOCK, blocks_c, BLOCK)
    return (shaped * flags.astype(weight.dtype)[:, None, :, None]).reshape(weight.shape)


def product_nn(left, right):
    return jnp.dot(left, right, preferred_element_type=jnp.float32)


def product_nt(left, right):
    return lax.dot_general(
        left, right, (((1,), (1,)), ((), ())), preferred_element_type=jnp.float32
    )


def product_tn(left, right):
    return lax.dot_general(
        left, right, (((0,), (0,)), ((), ())), preferred_element_type=jnp.float32
    )


def row_gather(value):
    return lax.all_gather(value, "row", axis=0, tiled=True)


def col_gather(value):
    return lax.all_gather(value, "col", axis=0, tiled=True)


def row_sum(panel):
    return lax.psum_scatter(panel.astype(jnp.bfloat16), "row", scatter_dimension=0, tiled=True)


def col_sum(panel):
    return lax.psum_scatter(panel, "col", scatter_dimension=0, tiled=True).astype(jnp.float32)


def after(value, *others):
    return lax.optimization_barrier((value,) + others)[0]


def local(
    resid_in,
    attn_out,
    cotangent,
    w_out,
    w_gate,
    w_up,
    w_down,
    mask_out,
    mask_gate,
    mask_up,
    mask_down,
):
    f32 = jnp.float32
    bf16 = jnp.bfloat16
    units = w_gate.shape[1]
    part = units // CHUNKS
    flag_part = part // BLOCK
    pruned_out = expand(w_out, mask_out)
    pruned_down = expand(w_down, mask_down)
    attn_full = row_gather(attn_out)
    upstream = col_gather(cotangent)
    projected = col_sum(product_nn(attn_full, pruned_out))
    hidden_part = product_nt(upstream, pruned_down).astype(bf16)
    hidden_grad = row_gather(row_sum(hidden_part))
    projected = after(projected, hidden_part)
    resid = (resid_in.astype(f32) + projected).astype(bf16)
    resid_full = col_gather(resid)
    resid_full = after(resid_full, hidden_grad)
    pairs, values = [], []
    for j in range(CHUNKS):
        cols = slice(j * part, (j + 1) * part)
        flags = slice(j * flag_part, (j + 1) * flag_part)
        pair = jnp.concatenate(
            [expand(w_gate[:, cols], mask_gate[:, flags]), expand(w_up[:, cols], mask_up[:, flags])], 1
        )
        pairs.append(pair)
        values.append(row_gather(row_sum(product_nn(resid_full, pair))))
    returned, lowered = 0.0, 0.0
    grads = []
    for j in range(CHUNKS):
        pair_val = values[j].astype(f32)
        gate_val, up_val = pair_val[:, :part], pair_val[:, part:]
        upper = hidden_grad[:, j * part : (j + 1) * part].astype(f32)
        logistic = jax.nn.sigmoid(gate_val)
        hidden = (gate_val * logistic * up_val).astype(bf16)
        gate_grad = (upper * up_val * logistic * (1.0 + gate_val * (1.0 - logistic))).astype(bf16)
        up_grad = (upper * gate_val * logistic).astype(bf16)
        grads.append((hidden, gate_grad, up_grad))
        returned = returned + product_nt(gate_grad, pairs[j][:, :part]) + product_nt(up_grad, pairs[j][:, part:])
        lowered = lowered + product_nn(hidden, pruned_down[j * part : (j + 1) * part])
    grad_resid = (cotangent.astype(f32) + col_sum(returned.astype(bf16))).astype(bf16)
    grad_full = col_gather(grad_resid)
    layer_out = (resid.astype(f32) + col_sum(after(lowered.astype(bf16), grad_full))).astype(bf16)
    grad_attn = row_sum(product_nt(grad_full, pruned_out))
    gates, ups, downs = [], [], []
    for j in range(CHUNKS):
        flags = slice(j * flag_part, (j + 1) * flag_part)
        hidden, gate_grad, up_grad = grads[j]
        gates.append(expand(product_tn(resid_full, gate_grad), mask_gate[:, flags]).astype(bf16))
        ups.append(expand(product_tn(resid_full, up_grad), mask_up[:, flags]).astype(bf16))
        downs.append(expand(product_tn(hidden, upstream), mask_down[flags]).astype(bf16))
    grad_w_gate = jnp.concatenate(gates, 1)
    grad_w_up = jnp.concatenate(ups, 1)
    grad_w_down = jnp.concatenate(downs, 0)
    grad_w_out = expand(product_tn(attn_full, grad_full), mask_out).astype(bf16)
    return (layer_out, grad_resid, grad_attn, grad_w_out, grad_w_gate, grad_w_up, grad_w_down)


def solution(mesh):
    placed = (
        P("col", "row"),
        P("row", "col"),
        P("col", "row"),
        P("col", "row"),
        P("row", "col"),
        P("row", "col"),
        P("col", "row"),
        P("col", "row"),
        P("row", "col"),
        P("row", "col"),
        P("col", "row"),
    )
    return jax.shard_map(
        local,
        mesh=mesh,
        in_specs=placed,
        out_specs=(
            P("col", "row"),
            P("col", "row"),
            P("row", "col"),
            P("col", "row"),
            P("row", "col"),
            P("row", "col"),
            P("col", "row"),
        ),
        check_vma=False,
    )
```

time: 743 us -> 677 us (0.911); the launches traced: 743 us -> 668 us
  waiting for transfers between devices: 594 us -> 479 us
  local copies, waits for them, and re-layouts: 17.7 us -> 43.2 us
  starting transfers between devices: 0.67 us -> 12.7 us
    reduce_scatter x6, waiting for transfers between devices: 363 us -> 229 us  [the longest x4 152 us: row_sum(): lax.psum_scatter(panel.astype(jnp.bfloat16), 'row', scatter_dimension=0,...]
    all_gather x2 -> x4, waiting for transfers between devices: 118 us -> 186 us  [row_gather(): return lax.all_gather(value, 'row', axis=0, tiled=True)]
    all_gather x1 -> x0, waiting for transfers between devices: 51.6 us -> none  [local(): hidden_full = lax.all_gather(hidden, 'row', axis=0, tiled=True)]
    unnamed x33 -> x69, local copies, waits for them, and re-layouts: 9.99 us -> 37.8 us
    reduce_scatter x6, starting transfers between devices: 0.25 us -> 12 us  [the longest x4 11.9 us: row_sum(): lax.psum_scatter(panel.astype(jnp.bfloat16), 'row', scatter_dimension=0,...]
    dot_general x3 -> x6, matrix products: 28 us -> 34.5 us  [product_nt(): lax.dot_general(left, right, (((1,), (1,)), ((), ())), preferred_element_...]
    dot_general x3 -> x7, matrix products: 23.7 us -> 19.3 us  [product_tn(): lax.dot_general(left, right, (((0,), (0,)), ((), ())), preferred_element_...]
    dot_general x3 -> x5, matrix products: 32.4 us -> 29.6 us  [product_nn(): return jnp.dot(left, right, preferred_element_type=jnp.float32)]
  transfers between devices with their start and end apart: 12 -> 14, of which waited for: 12 -> 13; matrix products, arithmetic and copies ran while one was open for 13% -> 15% of each run, Pallas kernels for 0% -> 0%
where the time goes in v1:
time: 677 us; the launch traced here: 668 us
  waiting for transfers between devices  479 us (71%)
  matrix products  83.3 us (12%)
  local copies, waits for them, and re-layouts  43.2 us (6%)
  other arithmetic  34.9 us (5%)
  between operations  14.5 us (2%)
  starting transfers between devices  12.7 us (2%)
    all_gather x4, waiting for transfers between devices, row_gather(): return lax.all_gather(value, 'row', axis=0, tiled=True)  186 us
    reduce_scatter x4, waiting for transfers between devices, row_sum(): lax.psum_scatter(panel.astype(jnp.bfloat16), 'row', scatter_dimension=0,...  152 us
    reduce_scatter x2, waiting for transfers between devices, col_sum(): lax.psum_scatter(panel, 'col', scatter_dimension=0, tiled=True)  76.9 us
    all_gather x3, waiting for transfers between devices, col_gather(): return lax.all_gather(value, 'col', axis=0, tiled=True)  62.7 us
    unnamed x69, local copies, waits for them, and re-layouts  37.8 us
    dot_general x6, matrix products, product_nt(): lax.dot_general(left, right, (((1,), (1,)), ((), ())), preferred_element_...  34.5 us
    dot_general x5, matrix products, product_nn(): return jnp.dot(left, right, preferred_element_type=jnp.float32)  29.6 us
    dot_general x7, matrix products, product_tn(): lax.dot_general(left, right, (((0,), (0,)), ((), ())), preferred_element_...  19.3 us
  transfers between devices with their start and end apart: 14, of which 13 were waited for; matrix products, arithmetic and copies ran while one was open for 15% of the time, Pallas kernels for 0%

profile of v1, /device:TPU:0, one launch (start us, length us, event | category | flops | bytes accessed | tf_op | source)
XLA Modules:
  0.0 667.9 jit_solution(7114572748308854411)
XLA Ops:
  9.5 29.7 %all-gather.8.cloned.1.call-done = bf16[1024,512]{1,0:T(8,128)(2,1)} async-done(((bf16[256,512]{1,0:T(8,128)(2,1)}), bf16[1024,512]{1,0:T(8,128)(2,1)}) %all-gather.8.cloned.1.call-update) | async-done | bytes 1048592 | tf_op jit(solution)/shard_map/all_gather | solution.py:34
  39.4 4.9 convolution_bitcast_fusion
  45.1 24.9 %all-gather.10.cloned.1.call-done = bf16[1024,1024]{1,0:T(8,128)(2,1)} async-done(((bf16[128,1024]{1,0:T(8,128)(2,1)}), bf16[1024,1024]{1,0:T(8,128)(2,1)}) %all-gather.10.cloned.1.call-update) | async-done | bytes 2097168 | tf_op jit(solution)/shard_map/all_gather | solution.py:38
  70.5 1.6 copy-done.4
  72.1 7.7 %convert_bitcast_fusion = bf16[1024,2048]{0,1:T(8,128)(2,1)} fusion(bf16[1024,1024]{1,0:T(8,128)(2,1)} %all-gather.10.cloned.1.call-done, bf16[2048,1024]{1,0:T(8,128)(2,1)S(1)} %copy-done.4, bf16[256,8,8,128]{3,2,1,0:T(8,128)(2,1)S(1)} %bitcast.147), kind=kOutput, calls=%fused_computation.47 | convolution fusion | flops 4299161600 | bytes 14680064 | tf_op jit(solution)/shard_map/dot_general | solution.py:22
  80.9 41.4 %reduce-scatter.10.cloned.1.call-done = f32[128,1024]{0,1:T(8,128)} async-done(((f32[1024,1024]{0,1:T(8,128)}), f32[128,1024]{0,1:T(8,128)}) %reduce-scatter.10.cloned.1.call-update) | async-done | bytes 524304 | tf_op jit(solution)/shard_map/reduce_scatter | solution.py:46
  122.3 1.8 add_convert_fusion.4
  124.2 52.4 %reduce-scatter.12.cloned.1.call-done = bf16[256,2048]{0,1:T(8,128)(2,1)} async-done(((bf16[1024,2048]{0,1:T(8,128)(2,1)}), bf16[256,2048]{0,1:T(8,128)(2,1)}) %reduce-scatter.12.cloned.1.call-update) | async-done | bytes 1048592 | tf_op jit(solution)/shard_map/reduce_scatter | solution.py:42
  180.3 3.0 bitcast_multiply_fusion.14
  183.3 26.2 %all-gather.12.cloned.1.call-done = bf16[1024,1024]{0,1:T(8,128)(2,1)} async-done(((bf16[128,1024]{0,1:T(8,128)(2,1)}), bf16[1024,1024]{0,1:T(8,128)(2,1)}) %all-gather.12.cloned.1.call-update) | async-done | bytes 2097168 | tf_op jit(solution)/shard_map/all_gather | solution.py:38
  209.5 53.5 %all-gather.14.cloned.1.call-done = bf16[1024,2048]{0,1:T(8,128)(2,1)} async-done(((bf16[256,2048]{0,1:T(8,128)(2,1)}), bf16[1024,2048]{0,1:T(8,128)(2,1)}) %all-gather.14.cloned.1.call-update) | async-done | bytes 4194320 | tf_op jit(solution)/shard_map/all_gather | solution.py:34
  263.0 9.4 %fusion.29 = bf16[1024,2048]{0,1:T(8,128)(2,1)} fusion(bf16[1024,1024]{0,1:T(8,128)(2,1)} %all-gather.12.cloned.1.call-done, bf16[1024,1024]{1,0:T(8,128)(2,1)} %get-tuple-element.38, bf16[1024,1024]{1,0:T(8,128)(2,1)} %get-tuple-element.53), kind=kOutput, calls=%fused_computation.49 | convolution fusion | flops 4305453056 | bytes 10485760 | tf_op jit(solution)/shard_map/dot_general | solution.py:18
  272.5 11.8 %reduce-scatter.16.cloned.1.call-start = ((), (), s32[]{:S(2)}) async-start(), calls=%async_computation.15 | async-start | bytes 5242880 | tf_op jit(solution)/shard_map/reduce_scatter | solution.py:42
  284.2 9.1 %fusion.26 = bf16[1024,2048]{0,1:T(8,128)(2,1)} fusion(bf16[1024,1024]{0,1:T(8,128)(2,1)} %all-gather.12.cloned.1.call-done, bf16[1024,1024]{1,0:T(8,128)(2,1)S(1)} %get-tuple-element.39, bf16[1024,1024]{1,0:T(8,128)(2,1)} %get-tuple-element.52), kind=kOutput, calls=%fused_computation.48 | convolution fusion | flops 4305453056 | bytes 10485760 | tf_op jit(solution)/shard_map/dot_general | solution.py:18
  293.4 31.9 %reduce-scatter.14.cloned.1.call-done = bf16[256,2048]{0,1:T(8,128)(2,1)} async-done(((bf16[1024,2048]{0,1:T(8,128)(2,1)}), bf16[256,2048]{0,1:T(8,128)(2,1)}) %reduce-scatter.14.cloned.1.call-update) | async-done | bytes 1048592 | tf_op jit(solution)/shard_map/reduce_scatter | solution.py:42
  325.4 56.2 %reduce-scatter.16.cloned.1.call-done = bf16[256,2048]{0,1:T(8,128)(2,1)} async-done(((bf16[1024,2048]{0,1:T(8,128)(2,1)}), bf16[256,2048]{0,1:T(8,128)(2,1)}) %reduce-scatter.16.cloned.1.call-update) | async-done | bytes 1048592 | tf_op jit(solution)/shard_map/reduce_scatter | solution.py:42
  381.6 54.5 %all-gather.16.cloned.1.call-done = bf16[1024,2048]{0,1:T(8,128)(2,1)} async-done(((bf16[256,2048]{0,1:T(8,128)(2,1)}), bf16[1024,2048]{0,1:T(8,128)(2,1)}) %all-gather.16.cloned.1.call-update) | async-done | bytes 4194320 | tf_op jit(solution)/shard_map/all_gather | solution.py:34
  436.1 6.5 convert_element_type.145
  442.6 47.9 %all-gather.18.cloned.1.call-done = bf16[1024,2048]{0,1:T(8,128)(2,1)} async-done(((bf16[256,2048]{0,1:T(8,128)(2,1)}), bf16[1024,2048]{0,1:T(8,128)(2,1)}) %all-gather.18.cloned.1.call-update) | async-done | bytes 4194320 | tf_op jit(solution)/shard_map/all_gather | solution.py:34
  490.5 3.4 convert_element_type.150
  496.4 7.3 %fusion.4 = (bf16[1024,1024]{0,1:T(8,128)(2,1)}, bf16[1024,1024]{0,1:T(8,128)(2,1)}, bf16[1024,1024]{0,1:T(8,128)(2,1)}, bf16[1024,1024]{0,1:T(8,128)(2,1)}, bf16[1024,1024]{0,1:T(8,128)(2,1)}) fusion(f32[1024,2048]{0,1:T(8,128)S(1)} %copy-done.1, bf16[1024,2048]{0,1:T(8,128)(2,1)S(1)} %copy-done.2, f32[1024,2048]{0,1:T(8,128)S(1)} %convert_element_type.150), kind=kLoop, calls=%fused_computation.8 | loop fusion | flops 32505856 | bytes 31457280 | tf_op jit(solution)/shard_map/convert_element_type | solution.py:100
  503.7 6.8 %fusion.49 = f32[1024,1024]{1,0:T(8,128)} fusion(bf16[1024,1024]{0,1:T(8,128)(2,1)} %get-tuple-element.33, bf16[1024,1024]{1,0:T(8,128)(2,1)} %get-tuple-element.52), kind=kOutput, calls=%fused_computation.84 | convolution fusion | flops 2147483648 | bytes 8388608 | tf_op jit(solution)/shard_map/dot_general | solution.py:22
  510.4 4.4 fusion.47
  514.9 4.4 fusion.48
  519.3 7.1 %add_convert_fusion = bf16[1024,1024]{1,0:T(8,128)(2,1)} fusion(f32[1024,1024]{1,0:T(8,128)} %fusion.49, f32[1024,1024]{1,0:T(8,128)} %fusion.47, f32[1024,1024]{1,0:T(8,128)} %fusion.48, bf16[1024,1024]{1,0:T(8,128)(2,1)S(1)} %copy-done.9, f32[1024,2048]{0,1:T(8,128)S(1)} %convert_element_type.150, bf16[1024,2048]{0,1:T(8,128)(2,1)S(1)} %copy-done.2), kind=kOutput, calls=%fused_computation.41 | convolution fusion | flops 2159017984 | bytes 23068672 | tf_op jit(solution)/shard_map/dot_general | solution.py:22
  526.9 35.5 %reduce-scatter.18.cloned.1.call-done = bf16[128,1024]{1,0:T(8,128)(2,1)} async-done(((bf16[1024,1024]{1,0:T(8,128)(2,1)}), bf16[128,1024]{1,0:T(8,128)(2,1)}) %reduce-scatter.18.cloned.1.call-update) | async-done | bytes 262160 | tf_op jit(solution)/shard_map/reduce_scatter | solution.py:46
  562.4 1.7 add_convert_fusion.3
  564.2 5.3 copy.59
  570.1 2.7 bitcast_multiply_fusion.6
  574.4 2.4 fusion.33
  576.8 3.8 add_convert_fusion.1
  580.6 11.6 %all-gather.20.cloned.1.call-done = bf16[1024,1024]{1,0:T(8,128)(2,1)} async-done(((bf16[128,1024]{1,0:T(8,128)(2,1)}), bf16[1024,1024]{1,0:T(8,128)(2,1)}) %all-gather.20.cloned.1.call-update) | async-done | bytes 2097168 | tf_op jit(solution)/shard_map/all_gather | solution.py:38
  594.5 2.6 fusion.14
  598.7 2.6 fusion.15
  601.2 2.5 pad_maximum_fusion
  603.7 6.6 copy.49
  610.7 5.0 fusion.13
  616.0 1.9 copy-done.3
  617.9 2.8 fusion.12
  620.7 2.5 pad_maximum_fusion.1
  623.2 6.4 copy.50
  629.6 4.1 convolution_convert_fusion
  636.0 2.5 fusion.10
  638.9 2.6 fusion.11
  641.5 2.5 pad_maximum_fusion.2
  644.6 1.3 fusion.32
  645.8 1.3 copy.48
  649.2 12.0 %reduce-scatter.20.cloned.1.call-done = bf16[256,512]{1,0:T(8,128)(2,1)} async-done(((bf16[1024,512]{1,0:T(8,128)(2,1)}), bf16[256,512]{1,0:T(8,128)(2,1)}) %reduce-scatter.20.cloned.1.call-update) | async-done | bytes 262160 | tf_op jit(solution)/shard_map/reduce_scatter | solution.py:42
  (120 shorter events, 23.7 us)
Async XLA Ops:
  7.2 32.0 %all-gather.8.cloned.1.call-start = ((), (), s32[]{:S(2)}) async-start(), calls=%async_computation.7 | async-start | bytes 1310720 | tf_op jit(solution)/shard_map/all_gather | solution.py:34
  7.9 62.0 %all-gather.10.cloned.1.call-start = ((), (), s32[]{:S(2)}) async-start(), calls=%async_computation.9 | async-start | bytes 2359296 | tf_op jit(solution)/shard_map/all_gather | solution.py:38
  8.6 113.7 %reduce-scatter.10.cloned.1.call-start = ((), (), s32[]{:S(2)}) async-start(), calls=%async_computation.8 | async-start | bytes 4718592 | tf_op jit(solution)/shard_map/reduce_scatter | solution.py:46
  44.3 0.7 copy-start.22
  44.3 132.3 %reduce-scatter.12.cloned.1.call-start = ((), (), s32[]{:S(2)}) async-start(), calls=%async_computation.11 | async-start | bytes 5242880 | tf_op jit(solution)/shard_map/reduce_scatter | solution.py:42
  69.9 2.2 copy-start.4
  79.8 0.9 copy-start.21
  79.8 96.9 %copy-start.23 = (s32[8,16]{1,0:T(8,128)S(1)}, s32[8,16]{1,0:T(8,128)}, u32[]{:S(2)}) copy-start(s32[8,16]{1,0:T(8,128)} %param.20) | copy-start | bytes 1540
  79.8 97.0 %copy-start.24 = (s32[8,16]{1,0:T(8,128)S(1)}, s32[8,16]{1,0:T(8,128)}, u32[]{:S(2)}) copy-start(s32[8,16]{1,0:T(8,128)} %param.19) | copy-start | bytes 1540
  79.8 129.7 %all-gather.12.cloned.1.call-start = ((), (), s32[]{:S(2)}) async-start(), calls=%async_computation.10 | async-start | bytes 2359296 | tf_op jit(solution)/shard_map/all_gather | solution.py:38
  124.2 138.8 %all-gather.14.cloned.1.call-start = ((), (), s32[]{:S(2)}) async-start(), calls=%async_computation.12 | async-start | bytes 5242880 | tf_op jit(solution)/shard_map/all_gather | solution.py:34
  176.6 148.7 %reduce-scatter.14.cloned.1.call-start = ((), (), s32[]{:S(2)}) async-start(), calls=%async_computation.13 | async-start | bytes 5242880 | tf_op jit(solution)/shard_map/reduce_scatter | solution.py:42
  176.8 2.2 copy-start.5
  176.8 3.5 copy-start.6
  183.3 100.9 %copy-start.8 = (bf16[1024,1024]{1,0:T(8,128)(2,1)}, bf16[1024,1024]{1,0:T(8,128)(2,1)S(1)}, u32[]{:S(2)}) copy-start(bf16[1024,1024]{1,0:T(8,128)(2,1)S(1)} %get-tuple-element.39) | copy-start | bytes 6291460
  272.5 109.1 %reduce-scatter.16.cloned.1.call-start = ((), (), s32[]{:S(2)}) async-start(), calls=%async_computation.15 | async-start | bytes 5242880 | tf_op jit(solution)/shard_map/reduce_scatter | solution.py:42
  293.3 142.8 %all-gather.16.cloned.1.call-start = ((), (), s32[]{:S(2)}) async-start(), calls=%async_computation.14 | async-start | bytes 5242880 | tf_op jit(solution)/shard_map/all_gather | solution.py:34
  325.3 165.2 %all-gather.18.cloned.1.call-start = ((), (), s32[]{:S(2)}) async-start(), calls=%async_computation.16 | async-start | bytes 5242880 | tf_op jit(solution)/shard_map/all_gather | solution.py:34
  381.6 180.8 %reduce-scatter.18.cloned.1.call-start = ((), (), s32[]{:S(2)}) async-start(), calls=%async_computation.17 | async-start | bytes 2359296 | tf_op jit(solution)/shard_map/reduce_scatter | solution.py:46
  490.5 4.6 copy-start.1
  490.5 5.8 copy-start.2
  496.4 22.9 %copy-start = (f32[1024,2048]{0,1:T(8,128)}, f32[1024,2048]{0,1:T(8,128)S(1)}, u32[]{:S(2)}) copy-start(f32[1024,2048]{0,1:T(8,128)S(1)} %convert_element_type.150) | copy-start | bytes 25165828
  503.7 6.8 %copy-start.11 = (bf16[1024,1024]{1,0:T(8,128)(2,1)S(1)}, bf16[1024,1024]{1,0:T(8,128)(2,1)}, u32[]{:S(2)}) copy-start(bf16[1024,1024]{1,0:T(8,128)(2,1)} %get-tuple-element.53) | copy-start | bytes 6291460
  503.7 6.8 %copy-start.16 = (bf16[1024,1024]{0,1:T(8,128)(2,1)S(1)}, bf16[1024,1024]{0,1:T(8,128)(2,1)}, u32[]{:S(2)}) copy-start(bf16[1024,1024]{0,1:T(8,128)(2,1)} %get-tuple-element.28) | copy-start | bytes 6291460
  510.4 4.4 copy-start.10
  510.4 4.4 copy-start.15
  514.9 4.4 copy-start.9
  519.3 43.1 %copy-start.20 = (bf16[128,1024]{1,0:T(8,128)(2,1)S(1)}, bf16[128,1024]{1,0:T(8,128)(2,1)}, u32[]{:S(2)}) copy-start(bf16[128,1024]{1,0:T(8,128)(2,1)} %param.13) | copy-start | bytes 786436
  526.4 65.8 %all-gather.20.cloned.1.call-start = ((), (), s32[]{:S(2)}) async-start(), calls=%async_computation.18 | async-start | bytes 2359296 | tf_op jit(solution)/shard_map/all_gather | solution.py:38
  564.1 83.0 %reduce-scatter.22.cloned.1.call-start = ((), (), s32[]{:S(2)}) async-start(), calls=%async_computation.20 | async-start | bytes 2359296
  572.8 1.6 copy-start.13
  574.4 2.4 copy-start.12
  592.3 68.9 %reduce-scatter.20.cloned.1.call-start = ((), (), s32[]{:S(2)}) async-start(), calls=%async_computation.19 | async-start | bytes 1310720 | tf_op jit(solution)/shard_map/reduce_scatter | solution.py:42
  592.3 1.6 copy-start.18
  592.3 2.2 copy-start.26
  597.1 1.6 copy-start.17
  610.3 5.7 slice-start
  610.6 5.4 slice-start.1
  610.7 5.4 copy-start.27
  615.6 2.3 copy-start.3
  633.8 1.6 copy-start.14
  633.8 2.2 copy-start.25
  641.5 2.8 copy-start.19
  641.5 3.1 copy-start.28
  644.6 3.7 copy-start.7
Sparse Core Ops, SparseCore 0:
  9.8 29.3 all-gather.7
  40.8 29.0 all-gather.9
  72.8 49.4 reduce-scatter.9
  125.7 50.7 reduce-scatter.11
  178.7 30.8 all-gather.11
  211.4 51.6 all-gather.13
  272.6 52.6 reduce-scatter.13
  328.8 52.6 reduce-scatter.15
  383.5 52.5 all-gather.15
  437.9 52.5 all-gather.17
  526.6 35.7 reduce-scatter.17
  564.5 27.6 all-gather.19
  594.6 35.1 reduce-scatter.21
  633.9 27.2 reduce-scatter.19

commit v2 on v1

v2 whole, which is shorter than its diff:
```python
import jax
import jax.numpy as jnp
from jax import lax
from jax.sharding import PartitionSpec as P

BLOCK = 128


def expand(weight, flags):
    blocks_r = weight.shape[0] // BLOCK
    blocks_c = weight.shape[1] // BLOCK
    shaped = weight.reshape(blocks_r, BLOCK, blocks_c, BLOCK)
    return (shaped * flags.astype(weight.dtype)[:, None, :, None]).reshape(weight.shape)


def product_nn(left, right):
    return jnp.dot(left, right, preferred_element_type=jnp.float32)


def product_nt(left, right):
    return lax.dot_general(
        left, right, (((1,), (1,)), ((), ())), preferred_element_type=jnp.float32
    )


def product_tn(left, right):
    return lax.dot_general(
        left, right, (((0,), (0,)), ((), ())), preferred_element_type=jnp.float32
    )


def row_gather(value):
    return lax.all_gather(value, "row", axis=0, tiled=True)


def col_gather(value):
    return lax.all_gather(value, "col", axis=0, tiled=True)


def row_swap(value, step):
    count = lax.axis_size("row")
    return lax.ppermute(value, "row", [(i, i ^ step) for i in range(count)])


def row_gather_direct(value):
    count = lax.axis_size("row")
    me = lax.axis_index("row")
    rows = value.shape[0]
    full = jnp.zeros((rows * count, value.shape[1]), value.dtype)
    for step in range(count):
        block = row_swap(value, step) if step else value
        full = lax.dynamic_update_slice(full, block, ((me ^ step) * rows, 0))
    return full


def row_sum_direct(panel):
    count = lax.axis_size("row")
    me = lax.axis_index("row")
    rows = panel.shape[0] // count
    total = 0.0
    for step in range(count):
        block = lax.dynamic_slice_in_dim(panel, (me ^ step) * rows, rows, 0)
        if step:
            block = row_swap(block, step)
        total = total + block.astype(jnp.float32)
    return total


def row_sum(panel):
    return lax.psum_scatter(panel, "row", scatter_dimension=0, tiled=True)


def col_sum(panel):
    return lax.psum_scatter(panel, "col", scatter_dimension=0, tiled=True).astype(jnp.float32)


def after(value, *others):
    return lax.optimization_barrier((value,) + others)[0]


def local(
    resid_in,
    attn_out,
    cotangent,
    w_out,
    w_gate,
    w_up,
    w_down,
    mask_out,
    mask_gate,
    mask_up,
    mask_down,
):
    f32 = jnp.float32
    bf16 = jnp.bfloat16
    units = w_gate.shape[1]
    width = w_down.shape[1]
    pruned_out = expand(w_out, mask_out)
    pruned_down = expand(w_down, mask_down)
    pair = jnp.concatenate([expand(w_gate, mask_gate), expand(w_up, mask_up)], 1)
    attn_full = row_gather_direct(attn_out)
    upstream = col_gather(cotangent)
    projected = col_sum(product_nn(attn_full, pruned_out))
    hidden_part = product_nt(upstream, pruned_down).astype(bf16)
    hidden_grad = row_sum_direct(hidden_part)
    projected = after(projected, hidden_part)
    resid = (resid_in.astype(f32) + projected).astype(bf16)
    resid_full = col_gather(resid)
    resid_full = after(resid_full, hidden_grad)
    pair_val = row_sum(product_nn(resid_full, pair).astype(bf16)).astype(f32)
    gate_val, up_val = pair_val[:, :units], pair_val[:, units:]
    logistic = jax.nn.sigmoid(gate_val)
    hidden = (gate_val * logistic * up_val).astype(bf16)
    gate_grad = (hidden_grad * up_val * logistic * (1.0 + gate_val * (1.0 - logistic))).astype(bf16)
    up_grad = (hidden_grad * gate_val * logistic).astype(bf16)
    full = row_gather(jnp.concatenate([gate_grad, up_grad, hidden], 1))
    pair_grad, hidden_full = full[:, : 2 * units], full[:, 2 * units :]
    returned = product_nt(pair_grad, pair).astype(bf16)
    lowered = product_nn(hidden_full, pruned_down).astype(bf16)
    both = col_sum(jnp.concatenate([returned, lowered], 1))
    grad_resid = (cotangent.astype(f32) + both[:, :width]).astype(bf16)
    layer_out = (resid.astype(f32) + both[:, width:]).astype(bf16)
    grad_full = col_gather(grad_resid)
    grad_attn = row_sum_direct(product_nt(grad_full, pruned_out).astype(bf16)).astype(bf16)
    grad_w_gate = expand(product_tn(resid_full, pair_grad[:, :units]), mask_gate).astype(bf16)
    grad_w_up = expand(product_tn(resid_full, pair_grad[:, units:]), mask_up).astype(bf16)
    grad_w_down = expand(product_tn(hidden_full, upstream), mask_down).astype(bf16)
    grad_w_out = expand(product_tn(attn_full, grad_full), mask_out).astype(bf16)
    return (layer_out, grad_resid, grad_attn, grad_w_out, grad_w_gate, grad_w_up, grad_w_down)


def solution(mesh):
    placed = (
        P("col", "row"),
        P("row", "col"),
        P("col", "row"),
        P("col", "row"),
        P("row", "col"),
        P("row", "col"),
        P("col", "row"),
        P("col", "row"),
        P("row", "col"),
        P("row", "col"),
        P("col", "row"),
    )
    return jax.shard_map(
        local,
        mesh=mesh,
        in_specs=placed,
        out_specs=(
            P("col", "row"),
            P("col", "row"),
            P("row", "col"),
            P("col", "row"),
            P("row", "col"),
            P("row", "col"),
            P("col", "row"),
        ),
        check_vma=False,
    )
```

time: 677 us -> 541 us (0.80)
  waiting for transfers between devices: 479 us -> 389 us
  local copies, waits for them, and re-layouts: 43.2 us -> 15.1 us
  other arithmetic: 34.9 us -> 19.2 us
    reduce_scatter x4 -> x1, waiting for transfers between devices: 152 us -> 85 us  [row_sum(): return lax.psum_scatter(panel, 'row', scatter_dimension=0, tiled=True)]
    all_gather x4 -> x1, waiting for transfers between devices: 186 us -> 122 us  [row_gather(): return lax.all_gather(value, 'row', axis=0, tiled=True)]
    ppermute x0 -> x9, waiting for transfers between devices: none -> 54.3 us  [row_swap(): return lax.ppermute(value, 'row', [(i, i ^ step) for i in range(count)])]
    all_gather x3, waiting for transfers between devices: 62.7 us -> 26.9 us  [col_gather(): return lax.all_gather(value, 'col', axis=0, tiled=True)]
    unnamed x69 -> x38, local copies, waits for them, and re-layouts: 37.8 us -> 8.37 us
    reduce_scatter x2, waiting for transfers between devices: 76.9 us -> 99.6 us  [col_sum(): lax.psum_scatter(panel, 'col', scatter_dimension=0, tiled=True)]
    dot_general x6 -> x3, matrix products: 34.5 us -> 20.7 us  [product_nt(): lax.dot_general(left, right, (((1,), (1,)), ((), ())), preferred_element_...]
    dot_general x7 -> x4, matrix products: 19.3 us -> 32.4 us  [product_tn(): lax.dot_general(left, right, (((0,), (0,)), ((), ())), preferred_element_...]
  transfers between devices with their start and end apart: 14 -> 16, of which waited for: 13 -> 13; matrix products, arithmetic and copies ran while one was open for 15% -> 10% of each run, Pallas kernels for 0% -> 0%
where the time goes in v2:
time: 541 us; the launch traced here: 531 us
  waiting for transfers between devices  389 us (72%)
  matrix products  80.8 us (15%)
  other arithmetic  19.2 us (4%)
  local copies, waits for them, and re-layouts  15.1 us (3%)
  between operations  14.9 us (3%)
  starting transfers between devices  12.3 us (2%)
    all_gather x1, waiting for transfers between devices, row_gather(): return lax.all_gather(value, 'row', axis=0, tiled=True)  122 us
    reduce_scatter x2, waiting for transfers between devices, col_sum(): lax.psum_scatter(panel, 'col', scatter_dimension=0, tiled=True)  99.6 us
    reduce_scatter x1, waiting for transfers between devices, row_sum(): return lax.psum_scatter(panel, 'row', scatter_dimension=0, tiled=True)  85 us
    ppermute x9, waiting for transfers between devices, row_swap(): return lax.ppermute(value, 'row', [(i, i ^ step) for i in range(count)])  54.3 us
    dot_general x4, matrix products, product_tn(): lax.dot_general(left, right, (((0,), (0,)), ((), ())), preferred_element_...  32.4 us
    dot_general x3, matrix products, product_nn(): return jnp.dot(left, right, preferred_element_type=jnp.float32)  27.7 us
    all_gather x3, waiting for transfers between devices, col_gather(): return lax.all_gather(value, 'col', axis=0, tiled=True)  26.9 us
    dot_general x3, matrix products, product_nt(): lax.dot_general(left, right, (((1,), (1,)), ((), ())), preferred_element_...  20.7 us
  transfers between devices with their start and end apart: 16, of which 13 were waited for; matrix products, arithmetic and copies ran while one was open for 10% of the time, Pallas kernels for 0%

profile of v2, /device:TPU:0, one launch (start us, length us, event | category | flops | bytes accessed | tf_op | source)
XLA Modules:
  0.0 531.4 jit_solution(15940234539962548373)
XLA Ops:
  7.2 3.0 collective-permute-start
  10.2 1.5 collective-permute-start.1
  11.8 0.8 fusion.27
  12.6 1.0 constant_dynamic-update-slice_fusion.3
  13.6 4.0 collective-permute-done
  17.6 6.2 %collective-permute-done.1 = bf16[256,512]{1,0:T(8,128)(2,1)S(1)} collective-permute-done((bf16[256,512]{1,0:T(8,128)(2,1)}, bf16[256,512]{1,0:T(8,128)(2,1)S(1)}, u32[]{:S(2)}, u32[]{:S(2)}) %collective-permute-start.1) | collective-permute-done | bytes 262176 | tf_op jit(solution)/shard_map/ppermute | solution.py:42
  24.1 1.0 copy-done
  25.1 3.3 fusion.21
  28.4 0.7 all-gather.5.cloned.1.call-update
  29.2 49.7 %reduce-scatter.4.cloned.1.call-done = f32[128,1024]{1,0:T(8,128)} async-done(((f32[1024,1024]{1,0:T(8,128)}), f32[128,1024]{1,0:T(8,128)}) %reduce-scatter.4.cloned.1.call-update) | async-done | bytes 524304 | tf_op jit(solution)/shard_map/reduce_scatter | solution.py:74
  78.9 1.8 add_convert_fusion.1
  80.9 26.9 %all-gather.5.cloned.1.call-done = bf16[1024,1024]{1,0:T(8,128)(2,1)} async-done(((bf16[128,1024]{1,0:T(8,128)(2,1)}), bf16[1024,1024]{1,0:T(8,128)(2,1)}) %all-gather.5.cloned.1.call-update) | async-done | bytes 2097168 | tf_op jit(solution)/shard_map/all_gather | solution.py:37
  107.8 0.6 mul.139
  108.4 3.1 copy-done.15
  111.5 6.4 %convolution_convert_fusion.1 = bf16[2048,1024]{1,0:T(8,128)(2,1)S(1)} fusion(bf16[1024,1024]{1,0:T(8,128)(2,1)} %all-gather.5.cloned.1.call-done, bf16[2048,1024]{1,0:T(8,128)(2,1)S(1)} %copy-done.15, bf16[256,8,8,128]{3,2,1,0:T(8,128)(2,1)S(1)} %bitcast.72), kind=kOutput, calls=%fused_computation.16 | convolution fusion | flops 4299161600 | bytes 14680064 | tf_op jit(solution)/shard_map/dot_general | solution.py:21
  117.8 1.4 dynamic-slice_bitcast_fusion.2
  119.2 2.4 collective-permute-start.5
  122.7 0.6 mul.145
  123.3 0.6 mul.142
  123.9 1.0 copy-done.3
  124.9 1.3 copy-done.4
  126.2 4.3 bitcast_multiply_fusion.3
  130.5 15.8 %collective-permute-done.5 = bf16[256,2048]{0,1:T(8,128)(2,1)S(1)} collective-permute-done((bf16[256,2048]{0,1:T(8,128)(2,1)}, bf16[256,2048]{0,1:T(8,128)(2,1)S(1)}, u32[]{:S(2)}, u32[]{:S(2)}) %collective-permute-start.5) | collective-permute-done | bytes 1048608 | tf_op jit(solution)/shard_map/ppermute | solution.py:42
  146.4 21.7 %collective-permute-done.4 = bf16[256,2048]{0,1:T(8,128)(2,1)S(1)} collective-permute-done((bf16[256,2048]{0,1:T(8,128)(2,1)S(1)}, bf16[256,2048]{0,1:T(8,128)(2,1)S(1)}, u32[]{:S(2)}, u32[]{:S(2)}) %collective-permute-start.4) | collective-permute-done | bytes 1048608 | tf_op jit(solution)/shard_map/ppermute | solution.py:42
  168.3 1.7 fusion.12
  170.0 15.1 %convolution_convert_fusion = bf16[1024,4096]{0,1:T(8,128)(2,1)} fusion(bf16[1024,1024]{1,0:T(8,128)(2,1)} %all-gather.7.cloned.1.call-done, bf16[1024,2048]{1,0:T(8,128)(2,1)} %get-tuple-element.28, bf16[1024,2048]{1,0:T(8,128)(2,1)} %get-tuple-element.29), kind=kOutput, calls=%fused_computation.9 | convolution fusion | flops 8610906112 | bytes 18874368 | tf_op jit(solution)/shard_map/dot_general | solution.py:17
  185.3 85.0 %reduce-scatter.6.cloned.1.call-done = bf16[256,4096]{0,1:T(8,128)(2,1)} async-done(((bf16[1024,4096]{0,1:T(8,128)(2,1)}), bf16[256,4096]{0,1:T(8,128)(2,1)}) %reduce-scatter.6.cloned.1.call-update) | async-done | bytes 2097168 | tf_op jit(solution)/shard_map/reduce_scatter | solution.py:70
  270.3 1.9 convert_element_type.129
  272.2 1.6 multiply_convert_fusion.2
  273.8 1.8 pad_maximum_fusion.4
  275.6 122.5 %all-gather.9.cloned.1.call-done = bf16[1024,6144]{0,1:T(8,128)(2,1)} async-done(((bf16[256,6144]{0,1:T(8,128)(2,1)}), bf16[1024,6144]{0,1:T(8,128)(2,1)}) %all-gather.9.cloned.1.call-update) | async-done | bytes 12582928 | tf_op jit(solution)/shard_map/all_gather | solution.py:33
  398.1 9.4 %fusion.16 = bf16[1024,1024]{1,0:T(8,128)(2,1)S(1)} fusion(bf16[1024,6144]{0,1:T(8,128)(2,1)} %all-gather.9.cloned.1.call-done, bf16[2048,1024]{1,0:T(8,128)(2,1)} %param.17, bf16[256,8,8,128]{3,2,1,0:T(8,128)(2,1)} %bitcast.73), kind=kOutput, calls=%fused_computation.31 | convolution fusion | flops 4298113024 | bytes 14680064 | tf_op jit(solution)/shard_map/dot_general | solution.py:17
  407.5 11.3 %fusion.13 = bf16[1024,1024]{1,0:T(8,128)(2,1)S(1)} fusion(bf16[1024,2048]{1,0:T(8,128)(2,1)S(1)} %copy-done.5, bf16[1024,2048]{1,0:T(8,128)(2,1)S(1)} %copy-done.6, bf16[1024,6144]{0,1:T(8,128)(2,1)} %all-gather.9.cloned.1.call-done), kind=kOutput, calls=%fused_computation.30 | convolution fusion | flops 8607760384 | bytes 18874368 | tf_op jit(solution)/shard_map/dot_general | solution.py:21
  418.8 2.5 pad_maximum_fusion.3
  421.6 49.9 %reduce-scatter.8.cloned.1.call-done = bf16[128,2048]{1,0:T(8,128)(2,1)} async-done(((bf16[1024,2048]{1,0:T(8,128)(2,1)}), bf16[128,2048]{1,0:T(8,128)(2,1)}) %reduce-scatter.8.cloned.1.call-update) | async-done | bytes 524304 | tf_op jit(solution)/shard_map/reduce_scatter | solution.py:74
  471.5 1.1 convert_element_type.135
  472.6 0.9 fusion.19
  474.3 1.0 copy-done.17
  475.3 9.8 %fusion.2 = bf16[1024,2048]{1,0:T(8,128)(2,1)} fusion(f32[128,8,16,128]{3,2,1,0:T(8,128)S(1)} %bitcast.69, bf16[1024,1024]{1,0:T(8,128)(2,1)S(1)} %copy-done.17, bf16[1024,6144]{0,1:T(8,128)(2,1)} %all-gather.9.cloned.1.call-done), kind=kOutput, calls=%fused_computation.5 | convolution fusion | flops 4299161600 | bytes 18874368 | tf_op jit(solution)/shard_map/dot_general | solution.py:27
  485.7 9.9 %fusion.1 = bf16[1024,2048]{1,0:T(8,128)(2,1)} fusion(f32[128,8,16,128]{3,2,1,0:T(8,128)S(1)} %bitcast.68, bf16[1024,1024]{1,0:T(8,128)(2,1)S(1)} %copy-done.17, bf16[1024,6144]{0,1:T(8,128)(2,1)} %all-gather.9.cloned.1.call-done), kind=kOutput, calls=%fused_computation.3 | convolution fusion | flops 4299161600 | bytes 18874368 | tf_op jit(solution)/shard_map/dot_general | solution.py:27
  496.2 1.0 copy-done.16
  497.2 10.3 %fusion = bf16[2048,1024]{1,0:T(8,128)(2,1)} fusion(f32[256,8,8,128]{3,2,1,0:T(8,128)S(1)} %bitcast.67, bf16[1024,1024]{1,0:T(8,128)(2,1)S(1)} %copy-done.16, bf16[1024,6144]{0,1:T(8,128)(2,1)} %all-gather.9.cloned.1.call-done), kind=kOutput, calls=%fused_computation.1 | convolution fusion | flops 4299161600 | bytes 18874368 | tf_op jit(solution)/shard_map/dot_general | solution.py:27
  507.6 3.0 convolution_convert_fusion.2
  510.7 2.4 collective-permute-start.8
  514.5 2.4 fusion.10
  516.8 3.6 collective-permute-done.8
  520.4 2.7 collective-permute-done.7
  523.2 0.8 add_convert_fusion
  (70 shorter events, 6.0 us)
Async XLA Ops:
  7.2 17.9 %copy-start.8 = (bf16[512,1024]{1,0:T(8,128)(2,1)S(1)}, bf16[512,1024]{1,0:T(8,128)(2,1)}, u32[]{:S(2)}) copy-start(bf16[512,1024]{1,0:T(8,128)(2,1)} %param.14) | copy-start | bytes 3145732
  7.2 71.7 %reduce-scatter.4.cloned.1.call-start = ((), (), s32[]{:S(2)}) async-start(), calls=%async_computation.3 | async-start | bytes 4718592 | tf_op jit(solution)/shard_map/reduce_scatter | solution.py:74
  7.2 10.4 %collective-permute-start = (bf16[256,512]{1,0:T(8,128)(2,1)}, bf16[256,512]{1,0:T(8,128)(2,1)S(1)}, u32[]{:S(2)}, u32[]{:S(2)}) collective-permute-start(bf16[256,512]{1,0:T(8,128)(2,1)} %param.12), channel_id=1, source_target_pairs={{0,8},{8,0},{16,24},{24,16},{1,9},{9,1},{17,25},{25,17},{2,10},{10... | collective-permute-start | bytes 786440 | tf_op jit(solution)/shard_map/ppermute | solution.py:42
  10.2 13.6 %collective-permute-start.1 = (bf16[256,512]{1,0:T(8,128)(2,1)}, bf16[256,512]{1,0:T(8,128)(2,1)S(1)}, u32[]{:S(2)}, u32[]{:S(2)}) collective-permute-start(bf16[256,512]{1,0:T(8,128)(2,1)} %param.12), channel_id=1, source_target_pairs={{0,16},{8,24},{16,0},{24,8},{1,17},{9,25},{17,1},{25,9},{2,18},{10... | collective-permute-start | bytes 786440 | tf_op jit(solution)/shard_map/ppermute | solution.py:42
  11.7 12.1 %collective-permute-start.2 = (bf16[256,512]{1,0:T(8,128)(2,1)}, bf16[256,512]{1,0:T(8,128)(2,1)S(1)}, u32[]{:S(2)}, u32[]{:S(2)}) collective-permute-start(bf16[256,512]{1,0:T(8,128)(2,1)} %param.12), channel_id=1, source_target_pairs={{0,24},{8,16},{16,8},{24,0},{1,25},{9,17},{17,9},{25,1},{2,26},{10... | collective-permute-start | bytes 786440 | tf_op jit(solution)/shard_map/ppermute | solution.py:42
  24.1 1.0 copy-start
  28.4 50.5 %copy-start.11 = (bf16[128,1024]{1,0:T(8,128)(2,1)S(1)}, bf16[128,1024]{1,0:T(8,128)(2,1)}, u32[]{:S(2)}) copy-start(bf16[128,1024]{1,0:T(8,128)(2,1)} %param.11) | copy-start | bytes 786436
  28.4 52.4 %copy-start.12 = (s32[16,8]{0,1:T(8,128)S(1)}, s32[16,8]{0,1:T(8,128)}, u32[]{:S(2)}) copy-start(s32[16,8]{0,1:T(8,128)} %param.21) | copy-start | bytes 1540
  28.4 52.5 %copy-start.13 = (s32[8,16]{1,0:T(8,128)S(1)}, s32[8,16]{1,0:T(8,128)}, u32[]{:S(2)}) copy-start(s32[8,16]{1,0:T(8,128)} %param.20) | copy-start | bytes 1540
  28.4 52.5 %copy-start.14 = (s32[8,16]{1,0:T(8,128)S(1)}, s32[8,16]{1,0:T(8,128)}, u32[]{:S(2)}) copy-start(s32[8,16]{1,0:T(8,128)} %param.19) | copy-start | bytes 1540
  28.4 79.4 %all-gather.5.cloned.1.call-start = ((), (), s32[]{:S(2)}) async-start(), calls=%async_computation.4 | async-start | bytes 2359296 | tf_op jit(solution)/shard_map/all_gather | solution.py:37
  29.1 140.8 %all-gather.7.cloned.1.call-start = ((), (), s32[]{:S(2)}) async-start(), calls=%async_computation.5 | async-start | bytes 2359296 | tf_op jit(solution)/shard_map/all_gather | solution.py:37
  80.7 189.6 %reduce-scatter.6.cloned.1.call-start = ((), (), s32[]{:S(2)}) async-start(), calls=%async_computation.6 | async-start | bytes 10485760 | tf_op jit(solution)/shard_map/reduce_scatter | solution.py:70
  107.8 3.7 copy-start.15
  108.4 9.5 %copy-start.2 = (bf16[16,128,8,128]{3,2,1,0:T(8,128)(2,1)}, bf16[16,128,8,128]{3,2,1,0:T(8,128)(2,1)S(1)}, u32[]{:S(2)}) copy-start(bf16[16,128,8,128]{3,2,1,0:T(8,128)(2,1)S(1)} %mul.139) | copy-start | bytes 12582916
  119.2 27.1 %collective-permute-start.5 = (bf16[256,2048]{0,1:T(8,128)(2,1)}, bf16[256,2048]{0,1:T(8,128)(2,1)S(1)}, u32[]{:S(2)}, u32[]{:S(2)}) collective-permute-start(bf16[256,2048]{0,1:T(8,128)(2,1)} %get-tuple-element.13), channel_id=1, source_target_pairs={{0,24},{8,16},{16,8},{24,0},{1,25},{9,17},{17,9},{25,1},{2,26},{10... | collective-permute-start | bytes 3145736 | tf_op jit(solution)/shard_map/ppermute | solution.py:42
  121.6 46.5 %collective-permute-start.4 = (bf16[256,2048]{0,1:T(8,128)(2,1)S(1)}, bf16[256,2048]{0,1:T(8,128)(2,1)S(1)}, u32[]{:S(2)}, u32[]{:S(2)}) collective-permute-start(bf16[256,2048]{0,1:T(8,128)(2,1)S(1)} %get-tuple-element.14), channel_id=1, source_target_pairs={{0,16},{8,24},{16,0},{24,8},{1,17},{9,25},{17,1},{25,9},{2,18},{10... | collective-permute-start | bytes 3145736 | tf_op jit(solution)/shard_map/ppermute | solution.py:42
  122.1 46.1 %collective-permute-start.3 = (bf16[256,2048]{0,1:T(8,128)(2,1)S(1)}, bf16[256,2048]{0,1:T(8,128)(2,1)}, u32[]{:S(2)}, u32[]{:S(2)}) collective-permute-start(bf16[256,2048]{0,1:T(8,128)(2,1)S(1)} %get-tuple-element.12), channel_id=1, source_target_pairs={{0,8},{8,0},{16,24},{24,16},{1,9},{9,1},{17,25},{25,17},{2,10},{10... | collective-permute-start | bytes 3145736 | tf_op jit(solution)/shard_map/ppermute | solution.py:42
  122.7 2.2 copy-start.3
  122.7 3.5 copy-start.4
  185.1 213.0 %all-gather.9.cloned.1.call-start = ((), (), s32[]{:S(2)}) async-start(), calls=%async_computation.7 | async-start | bytes 15728640 | tf_op jit(solution)/shard_map/all_gather | solution.py:33
  275.6 195.9 %reduce-scatter.8.cloned.1.call-start = ((), (), s32[]{:S(2)}) async-start(), calls=%async_computation.8 | async-start | bytes 4718592 | tf_op jit(solution)/shard_map/reduce_scatter | solution.py:74
  398.1 9.4 %copy-start.5 = (bf16[1024,2048]{1,0:T(8,128)(2,1)S(1)}, bf16[1024,2048]{1,0:T(8,128)(2,1)}, u32[]{:S(2)}) copy-start(bf16[1024,2048]{1,0:T(8,128)(2,1)} %get-tuple-element.28) | copy-start | bytes 12582916
  398.1 9.4 %copy-start.6 = (bf16[1024,2048]{1,0:T(8,128)(2,1)S(1)}, bf16[1024,2048]{1,0:T(8,128)(2,1)}, u32[]{:S(2)}) copy-start(bf16[1024,2048]{1,0:T(8,128)(2,1)} %get-tuple-element.29) | copy-start | bytes 12582916
  421.3 51.3 %copy-start.7 = (bf16[128,1024]{1,0:T(8,128)(2,1)S(1)}, bf16[128,1024]{1,0:T(8,128)(2,1)}, u32[]{:S(2)}) copy-start(bf16[128,1024]{1,0:T(8,128)(2,1)} %add_convert_fusion.1) | copy-start | bytes 786436
  421.3 51.3 %copy-start.10 = (bf16[128,1024]{1,0:T(8,128)(2,1)S(1)}, bf16[128,1024]{1,0:T(8,128)(2,1)}, u32[]{:S(2)}) copy-start(bf16[128,1024]{1,0:T(8,128)(2,1)} %param.13) | copy-start | bytes 786436
  421.3 86.2 %all-gather.11.cloned.1.call-start = ((), (), s32[]{:S(2)}) async-start(), calls=%async_computation.9 | async-start | bytes 2359296 | tf_op jit(solution)/shard_map/all_gather | solution.py:37
  473.7 1.6 copy-start.17
  495.6 1.6 copy-start.16
  497.2 10.3 %copy-start.1 = (bf16[4,128,8,128]{3,2,1,0:T(8,128)(2,1)S(1)}, bf16[4,128,8,128]{3,2,1,0:T(8,128)(2,1)}, u32[]{:S(2)}) copy-start(bf16[4,128,8,128]{3,2,1,0:T(8,128)(2,1)} %copy-done) | copy-start | bytes 3145732
  497.2 10.3 %copy-start.9 = (bf16[512,1024]{1,0:T(8,128)(2,1)S(1)}, bf16[512,1024]{1,0:T(8,128)(2,1)}, u32[]{:S(2)}) copy-start(bf16[512,1024]{1,0:T(8,128)(2,1)} %param.14) | copy-start | bytes 3145732
  507.6 6.9 %copy-start.18 = (bf16[1024,1024]{1,0:T(8,128)(2,1)S(1)}, bf16[1024,1024]{1,0:T(8,128)(2,1)}, u32[]{:S(2)}) copy-start(bf16[1024,1024]{1,0:T(8,128)(2,1)} %all-gather.11.cloned.1.call-done) | copy-start | bytes 6291460
  510.7 9.8 %collective-permute-start.8 = (bf16[256,512]{1,0:T(8,128)(2,1)S(1)}, bf16[256,512]{1,0:T(8,128)(2,1)S(1)}, u32[]{:S(2)}, u32[]{:S(2)}) collective-permute-start(bf16[256,512]{1,0:T(8,128)(2,1)S(1)} %get-tuple-element.16), channel_id=1, source_target_pairs={{0,24},{8,16},{16,8},{24,0},{1,25},{9,17},{17,9},{25,1},{2,26},{10... | collective-permute-start | bytes 786440 | tf_op jit(solution)/shard_map/ppermute | solution.py:42
  513.1 10.1 %collective-permute-start.7 = (bf16[256,512]{1,0:T(8,128)(2,1)S(1)}, bf16[256,512]{1,0:T(8,128)(2,1)S(1)}, u32[]{:S(2)}, u32[]{:S(2)}) collective-permute-start(bf16[256,512]{1,0:T(8,128)(2,1)S(1)} %get-tuple-element.17), channel_id=1, source_target_pairs={{0,16},{8,24},{16,0},{24,8},{1,17},{9,25},{17,1},{25,9},{2,18},{10... | collective-permute-start | bytes 786440 | tf_op jit(solution)/shard_map/ppermute | solution.py:42
  513.7 9.6 %collective-permute-start.6 = (bf16[256,512]{1,0:T(8,128)(2,1)S(1)}, bf16[256,512]{1,0:T(8,128)(2,1)S(1)}, u32[]{:S(2)}, u32[]{:S(2)}) collective-permute-start(bf16[256,512]{1,0:T(8,128)(2,1)S(1)} %get-tuple-element.15), channel_id=1, source_target_pairs={{0,8},{8,0},{16,24},{24,16},{1,9},{9,1},{17,25},{25,17},{2,10},{10... | collective-permute-start | bytes 786440 | tf_op jit(solution)/shard_map/ppermute | solution.py:42
Sparse Core Ops, SparseCore 0:
  28.5 50.3 reduce-scatter.3
  80.5 27.2 all-gather.4
  109.9 28.5 all-gather.6
  185.2 85.0 reduce-scatter.5
  275.7 122.3 all-gather.8
  421.4 49.9 reduce-scatter.7
  473.7 27.2 all-gather.10
